TPU v7x, 256 devices: a whole 4x4x8 slice. The times are simulated.
256 devices in a mesh: grp: 4 (over x), ctx: 64 (over z, y, core).
Axes of the slice: x: 4, y: 4, z: 8, core: 2. Of those that a mesh axis runs over, the one named last changes fastest.
Arguments:
- queries: bfloat16 [32, 4, 16384], P('grp', None, 'ctx'), may hold values from -8 to 8
- prefix_kv: bfloat16 [8, 65536, 2048], P('grp', 'ctx'), may hold values from -16 to 16
- suffix_kv: bfloat16 [32, 1024, 2048], P('grp', 'ctx'), may hold values from -24 to 24
- new_kv: bfloat16 [32, 4, 2048], P('grp'), may hold values from -24 to 24
- prefix_id: int32 [32, 1], P('grp'), may hold values from 0 to 7; in each aligned block of 8 rows (0 to 7, 8 to 15, ...) at most 2 rows name the same one
- place: int32 [8], replicated, may hold values from 0 to 7, each once
- suffix_len: int32 [32], P('grp'), may hold values from 1 to 1024, 16384 in all
Outputs:
- attended: bfloat16 [32, 4, 16384], P('grp', None, 'ctx')
Inputs may be any that keep to these rules, and one draw needn't show every extreme that they name: `prefix_id`: among the 8 requests of one index of grp, at most 2 name the same prefix; some prefix is named by exactly 2 of them. `suffix_len`: some request has exactly 1024 cached positions.
All inputs are finite; a program needn't handle non-finite values. No bound on the sum of `suffix_len` on one device may be relied on, other than what follows from the above.
Results may differ from a plain program's by a relative error of at most 0.014.
Values may be sent and summed in bfloat16 or wider, within the bound.
No kernel may reach another device: no remote copies, remote signals or barrier semaphores. Data moves between devices by JAX's collectives and lax.ppermute only.
A program may use at most 320 MiB of HBM per device.

v0:
```python
import functools

import jax
import jax.numpy as jnp
from jax import lax
from jax.experimental import pallas as pl
from jax.experimental.pallas import tpu as pltpu
from jax.sharding import Mesh
from jax.sharding import PartitionSpec as P

GRP, NZ, NY, NC = 4, 8, 4, 2
HD = 128
STEPS = 4
REQ = 8
SPAN = 16
HALF = 1024
STATS = 32
ROWS = NZ * HD + STATS
TAIL = 32
MESSAGE = 4 * SPAN + 16
BACK = 40
ARRIVED = GRP * NZ * 32
CHUNK = 512
FACTOR = HD ** (-0.5) * 1.4426950408889634
NEG = -1e30
SMALL = 8 * 1024 * 1024
F32 = jnp.float32
BF16 = jnp.bfloat16


def nt_dot(a, b):
    return lax.dot_general(a, b, (((1,), (1,)), ((), ())), preferred_element_type=F32)


def tn_dot(a, b):
    return lax.dot_general(a, b, (((0,), (0,)), ((), ())), preferred_element_type=F32)


def slot_of(r, pid_ref, place_ref):
    chosen = [place_ref[pid_ref[i]] for i in range(r + 1)]
    rank = jnp.int32(0)
    for i in range(r):
        rank = rank + (chosen[i] == chosen[r]).astype(jnp.int32)
    return chosen[r] * 2 + rank


def pack_queries_kernel(pid_ref, place_ref, q_ref, send_ref, rows_ref, buf):
    buf[...] = jnp.zeros_like(buf)
    for pair in range(REQ // 2):
        both = []
        for r in (2 * pair, 2 * pair + 1):
            q = q_ref[r].astype(F32)
            rows = jnp.concatenate([q[:, :HD], q[:, HD:]], axis=0)
            buf[slot_of(r, pid_ref, place_ref)] = rows
            both.append(rows)
        rows_ref[pair] = jnp.concatenate(both, axis=0).astype(BF16)
    for g in range(GRP):
        block = buf[4 * g : 4 * g + 4].reshape(32, HD).astype(BF16)
        for z in range(NZ):
            send_ref[z * GRP + g] = block


def pack_queries(prefix_id, place, queries):
    return pl.pallas_call(
        pack_queries_kernel,
        out_shape=(
            jax.ShapeDtypeStruct((GRP * NZ, 32, HD), BF16),
            jax.ShapeDtypeStruct((REQ // 2, 16, HD), BF16),
        ),
        in_specs=[
            pl.BlockSpec(memory_space=pltpu.SMEM),
            pl.BlockSpec(memory_space=pltpu.SMEM),
            pl.BlockSpec(memory_space=pltpu.VMEM),
        ],
        out_specs=(
            pl.BlockSpec(memory_space=pltpu.VMEM),
            pl.BlockSpec(memory_space=pltpu.VMEM),
        ),
        scratch_shapes=[pltpu.VMEM((16, 8, HD), F32)],
        name="pack_queries",
    )(prefix_id, place, queries)


def pack_suffix_kernel(kv_ref, rows_ref, out_ref):
    for z in range(NZ):
        for y in range(NY):
            for r in range(2):
                for kind in range(2):
                    first = (2 * kind + r) * SPAN
                    block = kind * NZ + z
                    out_ref[y * NZ + z, first : first + SPAN, :] = kv_ref[
                        2 * y + r, :, block * HD : (block + 1) * HD
                    ]
            out_ref[y * NZ + z, 4 * SPAN :, :] = rows_ref[y]


def pack_suffix(suffix_kv, rows):
    return pl.pallas_call(
        pack_suffix_kernel,
        out_shape=jax.ShapeDtypeStruct((NZ * NY, MESSAGE, HD), BF16),
        in_specs=[pl.BlockSpec(memory_space=pltpu.VMEM)] * 2,
        out_specs=pl.BlockSpec(memory_space=pltpu.VMEM),
        compiler_params=pltpu.CompilerParams(vmem_limit_bytes=SMALL),
        name="pack_suffix",
    )(suffix_kv, rows)


def split_total(total):
    high = total.astype(BF16).astype(F32)
    return high, total - high


def lanes(block):
    return pl.ds(pl.multiple_of(block * HD, HD), HD)


def prefix_scores(queries, halves, z, p, score, peak):
    first = [pl.multiple_of((z * GRP + g) * 32 + p * 16, 16) for g in range(GRP)]
    q = jnp.concatenate([ref[pl.ds(row, 16), :] for ref in queries for row in first], axis=0)
    top = None
    for i, kv in enumerate(halves):
        for start in range(0, HALF, CHUNK):
            s = nt_dot(kv[p, start : start + CHUNK, lanes(z)], q)
            score[i * HALF + start : i * HALF + start + CHUNK, :] = s
            high = jnp.max(s.reshape(CHUNK // 8, 8, 256), axis=0)
            top = high if top is None else jnp.maximum(top, high)
    peak[...] = top


def prefix_values(halves, z, p, score, peak):
    top = jnp.max(peak[...], axis=0, keepdims=True) * FACTOR
    top = top.astype(BF16).astype(F32)
    total = jnp.zeros((8, 256), F32)
    summed = jnp.zeros((HD, 256), F32)
    for i, kv in enumerate(halves):
        for start in range(0, HALF, CHUNK):
            s = score[i * HALF + start : i * HALF + start + CHUNK, :]
            w = jnp.exp2(s * FACTOR - top)
            total = total + jnp.sum(w.reshape(CHUNK // 8, 8, 256), axis=0)
            v = kv[p, start : start + CHUNK, lanes(NZ + z)]
            summed = summed + tn_dot(v, w.astype(BF16))
    high, low = split_total(jnp.sum(total, axis=0, keepdims=True))
    return summed, (top, high, low)


def prefix_kernel(q0, q1, q2, q3, own, other, o0, o1, o2, o3, kv0, kv1, sa, sb, ma, mb, stats, sems):
    queries, halves = (q0, q1, q2, q3), (kv0, kv1)

    def fetch(half, kind, z):
        cols = lanes(kind * NZ + z)
        return pltpu.make_async_copy(
            (own, other)[half].at[:, :, cols], halves[half].at[:, :, cols], sems.at[half, kind, z]
        )

    for z in range(NZ):
        for kind in range(2):
            for half in range(2):
                fetch(half, kind, z).start()

    def ready(kind, z):
        fetch(0, kind, z).wait()
        fetch(1, kind, z).wait()

    def step(z, last):
        prefix_scores(queries, halves, z, 1, sb, mb)
        even = prefix_values(halves, z, 0, sa, ma)
        if not last:
            prefix_scores(queries, halves, z + 1, 0, sa, ma)
        odd = prefix_values(halves, z, 1, sb, mb)
        rows = pl.ds(pl.multiple_of(z * HD, HD), HD)
        for k, out in enumerate((o0, o1, o2, o3)):
            cols = slice(64 * k, 64 * (k + 1))
            out[rows, :] = jnp.concatenate([even[0][:, cols], odd[0][:, cols]], axis=1).astype(BF16)
            for i in range(3):
                stats[k, pl.ds(8 * i + z, 1), :] = jnp.concatenate(
                    [even[1][i][:, cols], odd[1][i][:, cols]], axis=1
                )

    stats[...] = jnp.zeros_like(stats)
    ready(0, 0)
    prefix_scores(queries, halves, 0, 0, sa, ma)

    def body(z, carry):
        ready(1, z)
        ready(0, z + 1)
        step(z, False)
        return carry

    lax.fori_loop(0, NZ - 1, body, 0)
    ready(1, NZ - 1)
    step(NZ - 1, True)
    for k, out in enumerate((o0, o1, o2, o3)):
        out[NZ * HD :, :] = stats[k].astype(BF16)


def prefix_attention(gathered, own, other):
    vmem = pl.BlockSpec(memory_space=pltpu.VMEM)
    hbm = pl.BlockSpec(memory_space=pl.ANY)
    return pl.pallas_call(
        prefix_kernel,
        out_shape=(jax.ShapeDtypeStruct((ROWS, HD), BF16),) * NY,
        in_specs=[vmem] * 4 + [hbm] * 2,
        out_specs=(vmem,) * NY,
        scratch_shapes=[
            pltpu.VMEM(own.shape, BF16),
            pltpu.VMEM(own.shape, BF16),
            pltpu.VMEM((2 * HALF, 256), F32),
            pltpu.VMEM((2 * HALF, 256), F32),
            pltpu.VMEM((8, 256), F32),
            pltpu.VMEM((8, 256), F32),
            pltpu.VMEM((NY, STATS, HD), F32),
            pltpu.SemaphoreType.DMA((2, 2, NZ)),
        ],
        compiler_params=pltpu.CompilerParams(vmem_limit_bytes=44 * 1024 * 1024),
        cost_estimate=pl.CostEstimate(
            flops=20 * 4096 * 2048 * HD, bytes_accessed=18 << 20, transcendentals=4096 * 2048
        ),
        name="prefix_attention",
    )(*gathered, own, other)


def suffix_kernel(len_ref, kv_own, kv_other, new_kv, o0, o1, o2, o3):
    y, z, core = lax.axis_index("y"), lax.axis_index("z"), lax.axis_index("c")
    index = lax.broadcasted_iota(jnp.int32, (32, 512), 1)
    source = index // SPAN
    base = (source % NZ * NY + source // NZ) * (2 * SPAN) + index % SPAN
    step = lax.broadcasted_iota(jnp.int32, (32, 1), 0) % STEPS
    sums, tops, totals = [], [], []
    queries = [
        kv_own[lax.rem(y + NY - k, NY) * NZ + z].astype(F32)[4 * SPAN :] for k in range(NY)
    ]
    for r in range(2):
        length = len_ref[2 * y + r]
        keys, values = slice(r * SPAN, (r + 1) * SPAN), slice((2 + r) * SPAN, (3 + r) * SPAN)
        qf = jnp.concatenate([q[8 * r : 8 * r + 8] for q in queries], axis=0)
        q = qf.astype(BF16)
        scores = []
        for ref, c in ((kv_own, core), (kv_other, 1 - core)):
            s = nt_dot(q, ref[:, keys, :].reshape(512, HD)) * FACTOR
            scores.append(jnp.where(base + c * SPAN < length, s, NEG))
        kn = new_kv[2 * y + r, :, lanes(z)].astype(F32)
        vn = new_kv[2 * y + r, :, lanes(NZ + z)].astype(F32)
        fresh = []
        for t in range(STEPS):
            s = jnp.sum(qf * kn[t : t + 1], axis=1, keepdims=True) * FACTOR
            fresh.append(jnp.where(step >= t, s, NEG))
        top = functools.reduce(
            jnp.maximum, [jnp.max(s, axis=1, keepdims=True) for s in scores] + fresh
        )
        top = top.astype(BF16).astype(F32)
        total = jnp.zeros((32, 1), F32)
        summed = jnp.zeros((32, HD), F32)
        for s, ref in zip(scores, (kv_own, kv_other)):
            w = jnp.exp2(s - top)
            total = total + jnp.sum(w, axis=1, keepdims=True)
            summed = summed + jnp.dot(
                w.astype(BF16), ref[:, values, :].reshape(512, HD), preferred_element_type=F32
            )
        for t in range(STEPS):
            w = jnp.exp2(fresh[t] - top)
            total = total + w
            summed = summed + w.astype(BF16).astype(F32) * vn[t : t + 1]
        sums.append(summed)
        tops.append(top)
        totals.append(total)
    lane = lax.broadcasted_iota(jnp.int32, (16, HD), 1)
    for k, out in enumerate((o0, o1, o2, o3)):
        rows = slice(8 * k, 8 * k + 8)
        top = jnp.concatenate([t[rows] for t in tops], axis=0)
        high, low = split_total(jnp.concatenate([t[rows] for t in totals], axis=0))
        out[:16, :] = jnp.concatenate([s[rows] for s in sums], axis=0).astype(BF16)
        stat = jnp.where(
            lane == 0, top, jnp.where(lane == 1, high, jnp.where(lane == 2, low, 0.0))
        )
        out[16:, :] = stat.astype(BF16)


def suffix_attention(lengths, kv_own, kv_other, new_kv):
    vmem = pl.BlockSpec(memory_space=pltpu.VMEM)
    return pl.pallas_call(
        suffix_kernel,
        in_specs=[pl.BlockSpec(memory_space=pltpu.SMEM)] + [vmem] * 3,
        out_specs=[vmem] * NY,
        out_shape=[jax.ShapeDtypeStruct((TAIL, HD), BF16)] * NY,
        cost_estimate=pl.CostEstimate(flops=1 << 20, bytes_accessed=1 << 16, transcendentals=0),
        compiler_params=pltpu.CompilerParams(vmem_limit_bytes=SMALL),
        name="suffix_attention",
    )(lengths, kv_own, kv_other, new_kv)


def combine_kernel(p0, p1, p2, p3, out_ref):
    stats = [ref[NZ * HD :, :].astype(F32) for ref in (p0, p1, p2, p3)]
    top = functools.reduce(jnp.maximum, [s[:NZ] for s in stats])
    factors = [jnp.exp2(s[:NZ] - top) for s in stats]
    total = sum((s[NZ : 2 * NZ] + s[2 * NZ : 3 * NZ]) * f for s, f in zip(stats, factors))
    high, low = split_total(total)
    row = lax.broadcasted_iota(jnp.int32, (8, HD), 0)
    for z in range(NZ):
        at = slice(z, z + 1)
        rows = slice(z * HD, (z + 1) * HD)
        summed = sum(ref[rows].astype(F32) * f[at] for ref, f in zip((p0, p1, p2, p3), factors))
        stat = jnp.where(
            row == 0, top[at], jnp.where(row == 1, high[at], jnp.where(row == 2, low[at], 0.0))
        )
        turned = jnp.transpose(summed)
        for g in range(GRP):
            out_ref[z * GRP + g] = jnp.concatenate(
                [turned[16 * g : 16 * g + 16], turned[64 + 16 * g : 80 + 16 * g], stat], axis=0
            ).astype(BF16)


def combine(parts):
    spec = pl.BlockSpec(memory_space=pltpu.VMEM)
    return pl.pallas_call(
        combine_kernel,
        out_shape=jax.ShapeDtypeStruct((GRP * NZ, BACK, HD), BF16),
        in_specs=[spec] * 4,
        out_specs=spec,
        compiler_params=pltpu.CompilerParams(vmem_limit_bytes=SMALL),
        name="combine",
    )(*parts)


def finish_kernel(pid_ref, place_ref, back_ref, t0, t1, t2, t3, out_ref, turned, sums, tops, totals, tails):
    y, g = lax.axis_index("y"), lax.axis_index("grp")
    for k, ref in enumerate((t0, t1, t2, t3)):
        tails[k] = ref[...].astype(F32)
    blocks = [back_ref[s].astype(F32) for s in range(GRP * NZ)]
    rows = []
    for src in range(GRP):
        stats = [b[32:BACK] for b in blocks[src::GRP]]
        top = functools.reduce(jnp.maximum, [s[0:1] for s in stats])
        factors = [jnp.exp2(s[0:1] - top) for s in stats]
        total = sum((s[1:2] + s[2:3]) * f for s, f in zip(stats, factors))
        rows += factors + [top, total, jnp.zeros((6, HD), F32)]
    rows.append(jnp.zeros((64, HD), F32))
    turned[...] = jnp.transpose(jnp.concatenate(rows, axis=0))
    cols = jnp.concatenate(
        [
            turned[pl.ds(pl.multiple_of(16 * g, 16), 16), :],
            turned[pl.ds(pl.multiple_of(64 + 16 * g, 16), 16), :],
        ],
        axis=0,
    )
    for src in range(GRP):
        col = [cols[:, 16 * src + i : 16 * src + i + 1] for i in range(10)]
        summed = sum(blocks[z * GRP + src][:32] * col[z] for z in range(NZ))
        sums[4 * src : 4 * src + 4] = summed.reshape(4, 8, HD)
        tops[4 * src : 4 * src + 4] = jnp.broadcast_to(col[8], (32, HD)).reshape(4, 8, HD)
        totals[4 * src : 4 * src + 4] = jnp.broadcast_to(col[9], (32, HD)).reshape(4, 8, HD)
    for r in range(REQ):
        slot = slot_of(r, pid_ref, place_ref)
        k = (r // 2 + NY - y) % NY
        tail = tails[k]
        base = 8 * (r % 2)
        s_sum = tail[base : base + 8]
        stat = tail[16 + base : 24 + base]
        s_top, s_total = stat[:, 0:1], stat[:, 1:2] + stat[:, 2:3]
        p_sum, p_top, p_total = sums[slot], tops[slot], totals[slot]
        top = jnp.maximum(p_top, s_top)
        left, right = jnp.exp2(p_top - top), jnp.exp2(s_top - top)
        result = (p_sum * left + s_sum * right) / (p_total * left + s_total * right)
        out_ref[r] = jnp.concatenate([result[:STEPS], result[STEPS:]], axis=1).astype(BF16)


def finish(prefix_id, place, back, tails):
    smem, vmem = (pl.BlockSpec(memory_space=space) for space in (pltpu.SMEM, pltpu.VMEM))
    return pl.pallas_call(
        finish_kernel,
        out_shape=jax.ShapeDtypeStruct((REQ, STEPS, 2 * HD), BF16),
        in_specs=[smem, smem] + [vmem] * 5,
        out_specs=vmem,
        scratch_shapes=[
            pltpu.VMEM((HD, HD), F32),
            pltpu.VMEM((16, 8, HD), F32),
            pltpu.VMEM((16, 8, HD), F32),
            pltpu.VMEM((16, 8, HD), F32),
            pltpu.VMEM((NY, TAIL, HD), F32),
        ],
        compiler_params=pltpu.CompilerParams(vmem_limit_bytes=SMALL),
        name="finish",
    )(prefix_id, place, back, *tails)


def turn(x, by):
    return lax.ppermute(x, "y", [(i, (i + by) % NY) for i in range(NY)])


def swap(x):
    return lax.ppermute(x, "c", [(0, 1), (1, 0)])


def per_device(queries, prefix_kv, suffix_kv, new_kv, prefix_id, place, suffix_len):
    other_kv = swap(prefix_kv)
    prefix_id = prefix_id.reshape(REQ)
    send, rows = pack_queries(prefix_id, place, queries)
    packed = pack_suffix(suffix_kv, rows)
    arrived = lax.all_to_all(send, ("z", "grp"), 0, 0, tiled=True)
    arrived, other_kv = lax.optimization_barrier((arrived, other_kv))
    arrived = arrived.reshape(ARRIVED, HD)
    gathered = [arrived] + [turn(arrived, k) for k in range(1, NY)]
    suffix_own = lax.all_to_all(packed, ("y", "z"), 0, 0, tiled=True)
    partials = list(prefix_attention(gathered, prefix_kv, other_kv))
    suffix_own, partials[0] = lax.optimization_barrier((suffix_own, partials[0]))
    parts = [partials[0]] + [turn(partials[k], -k) for k in range(1, NY)]
    suffix_other = swap(suffix_own)
    tails = suffix_attention(suffix_len, suffix_own, suffix_other, new_kv)
    tails = [tails[0]] + [turn(tails[k], -k) for k in range(1, NY)]
    joined = combine(parts)
    back = lax.all_to_all(joined, ("z", "grp"), 0, 0, tiled=True)
    return finish(prefix_id, place, back, tails)


def solution(mesh):
    inner = Mesh(mesh.devices.reshape(GRP, NZ, NY, NC), ("grp", "z", "y", "c"))
    ctx = ("z", "y", "c")
    return jax.shard_map(
        per_device,
        mesh=inner,
        in_specs=(
            P("grp", None, ctx),
            P("grp", ctx, None),
            P("grp", ctx, None),
            P("grp", None, None),
            P("grp", None),
            P(),
            P("grp"),
        ),
        out_specs=P("grp", None, ctx),
        check_vma=False,
    )
```

profile of v0, /device:TPU:4, one launch (start us, length us, event | category | flops | bytes accessed | tf_op | source)
XLA Modules:
  0.0 94.2 jit_solution(9777803599615393636)
XLA Ops:
  0.0 1.5 %pack_queries.1 = (bf16[32,32,128]{2,1,0:T(8,128)(2,1)}, bf16[4,16,128]{2,1,0:T(8,128)(2,1)}) custom-call(s32[8]{0:T(128)} %bitcast.6, s32[8]{0:T(128)} %place_ref.3, bf16[8,4,256]{2,1,0:T(4,128)(2,1)} %q_ref.1), custom_call_target="tpu_custom_call" | custom-call | tf_op jit(solution)/shard_map/pack_queries/pallas_call | solution.py:64
  1.5 23.5 %all_to_all.15 = bf16[32,32,128]{2,1,0:T(8,128)(2,1)S(1)} all-to-all(bf16[32,32,128]{2,1,0:T(8,128)(2,1)} %get-tuple-element.20), channel_id=1, replica_groups=mesh['grp'=4,'z'=8,'y'=4,'c'=2] {'z','grp'}, dimensions={0} | all-to-all | bytes 524288 | tf_op jit(solution)/shard_map/all_to_all | solution.py:398
  25.0 1.6 %collective-permute-start.1 = (bf16[1024,128]{1,0:T(8,128)(2,1)S(1)}, bf16[1024,128]{1,0:T(8,128)(2,1)S(1)}, u32[]{:S(2)}, u32[]{:S(2)}) collective-permute-start(bf16[1024,128]{1,0:T(8,128)(2,1)S(1)} %bitcast.2), channel_id=1, source_target_pairs={{0,2},{2,4},{4,6},{6,0},{1,3},{3,5},{5,7},{7,1},{8,10},{10,12},{12... | collective-permute-start | bytes 786440 | tf_op jit(solution)/shard_map/ppermute | solution.py:386
  26.6 2.9 %collective-permute-start.2 = (bf16[1024,128]{1,0:T(8,128)(2,1)S(1)}, bf16[1024,128]{1,0:T(8,128)(2,1)S(1)}, u32[]{:S(2)}, u32[]{:S(2)}) collective-permute-start(bf16[1024,128]{1,0:T(8,128)(2,1)S(1)} %bitcast.3), channel_id=1, source_target_pairs={{0,4},{2,6},{4,0},{6,2},{1,5},{3,7},{5,1},{7,3},{8,12},{10,14},{12... | collective-permute-start | bytes 786440 | tf_op jit(solution)/shard_map/ppermute | solution.py:386
  29.5 1.3 %collective-permute-start.3 = (bf16[1024,128]{1,0:T(8,128)(2,1)S(1)}, bf16[1024,128]{1,0:T(8,128)(2,1)S(1)}, u32[]{:S(2)}, u32[]{:S(2)}) collective-permute-start(bf16[1024,128]{1,0:T(8,128)(2,1)S(1)} %bitcast.4), channel_id=1, source_target_pairs={{0,6},{2,0},{4,2},{6,4},{1,7},{3,1},{5,3},{7,5},{8,14},{10,8},{12,... | collective-permute-start | bytes 786440 | tf_op jit(solution)/shard_map/ppermute | solution.py:386
  30.8 1.0 %copy-done = bf16[8,16,2048]{2,1,0:T(8,128)(2,1)S(1)} copy-done((bf16[8,16,2048]{2,1,0:T(8,128)(2,1)S(1)}, bf16[8,16,2048]{2,1,0:T(8,128)(2,1)}, u32[]{:S(2)}) %copy-start) | copy-done | bytes 524312
  31.9 0.7 copy-done.2
  32.6 1.0 %pack_suffix.1 = bf16[32,80,128]{2,1,0:T(8,128)(2,1)} custom-call(bf16[8,16,2048]{2,1,0:T(8,128)(2,1)S(1)} %copy-done, bf16[4,16,128]{2,1,0:T(8,128)(2,1)S(1)} %copy-done.2), custom_call_target="tpu_custom_call" | custom-call | tf_op jit(solution)/shard_map/pack_suffix/pallas_call | solution.py:98
  33.6 3.9 %all-to-all-start = ((bf16[32,80,128]{2,1,0:T(8,128)(2,1)}), bf16[32,80,128]{2,1,0:T(8,128)(2,1)S(1)}, u32[]{:S(2)}, u32[]{:S(2)}) async-start(bf16[32,80,128]{2,1,0:T(8,128)(2,1)} %pack_suffix.1), calls=%async_computation | async-start | bytes 1310720 | tf_op jit(solution)/shard_map/all_to_all | solution.py:402
  37.5 0.0 copy-start.1
  37.5 0.0 copy-start.5
  37.5 0.0 copy-start.3
  37.6 0.0 copy-start.4
  37.6 0.0 collective-permute-done.1.q1
  37.6 3.4 %collective-permute-done.2.q2 = bf16[1024,128]{1,0:T(8,128)(2,1)S(1)} collective-permute-done((bf16[1024,128]{1,0:T(8,128)(2,1)S(1)}, bf16[1024,128]{1,0:T(8,128)(2,1)S(1)}, u32[]{:S(2)}, u32[]{:S(2)}) %collective-permute-start.2) | collective-permute-done | bytes 262176 | tf_op jit(solution)/shard_map/ppermute | solution.py:386
  40.9 0.0 collective-permute-done.3.q3
  40.9 15.1 %prefix_attention.1 = (bf16[1056,128]{1,0:T(8,128)(2,1)S(1)}, bf16[1056,128]{1,0:T(8,128)(2,1)S(1)}, bf16[1056,128]{1,0:T(8,128)(2,1)S(1)}, bf16[1056,128]{1,0:T(8,128)(2,1)S(1)}) custom-call(bf16[1024,128]{1,0:T(8,128)(2,1)S(1)} %bitcast.5, bf16[1024,128]{1,0:T(8,128)(2,1)S(1)} %collective-permute-done.1.q1, ...), custom_call_target="tpu_custom_call" | custom-call | flops 21474836480 | bytes 18874368 | tf_op jit(solution)/shard_map/prefix_attention/pallas_call | solution.py:199
  56.1 2.4 %collective-permute-start.4 = (bf16[1056,128]{1,0:T(8,128)(2,1)S(1)}, bf16[1056,128]{1,0:T(8,128)(2,1)S(1)}, u32[]{:S(2)}, u32[]{:S(2)}) collective-permute-start(bf16[1056,128]{1,0:T(8,128)(2,1)S(1)} %get-tuple-element.25), channel_id=1, source_target_pairs={{0,6},{2,0},{4,2},{6,4},{1,7},{3,1},{5,3},{7,5},{8,14},{10,8},{12,... | collective-permute-start | bytes 811016 | tf_op jit(solution)/shard_map/ppermute | solution.py:386
  58.4 0.9 collective-permute-start.5
  59.4 0.8 collective-permute-start.6
  60.2 0.0 all-to-all-done.kv_own
  60.2 9.3 %collective-permute-done.4.p1 = bf16[1056,128]{1,0:T(8,128)(2,1)S(1)} collective-permute-done((bf16[1056,128]{1,0:T(8,128)(2,1)S(1)}, bf16[1056,128]{1,0:T(8,128)(2,1)S(1)}, u32[]{:S(2)}, u32[]{:S(2)}) %collective-permute-start.4) | collective-permute-done | bytes 270368 | tf_op jit(solution)/shard_map/ppermute | solution.py:386
  69.5 3.4 %collective-permute-done.6.p3 = bf16[1056,128]{1,0:T(8,128)(2,1)S(1)} collective-permute-done((bf16[1056,128]{1,0:T(8,128)(2,1)S(1)}, bf16[1056,128]{1,0:T(8,128)(2,1)S(1)}, u32[]{:S(2)}, u32[]{:S(2)}) %collective-permute-start.6) | collective-permute-done | bytes 270368 | tf_op jit(solution)/shard_map/ppermute | solution.py:386
  72.9 1.0 %combine.1 = bf16[32,40,128]{2,1,0:T(8,128)(2,1)} custom-call(bf16[1056,128]{1,0:T(8,128)(2,1)S(1)} %get-tuple-element.24.p0, bf16[1056,128]{1,0:T(8,128)(2,1)S(1)} %collective-permute-done.4.p1, bf16[1056,128]{1,0:T(8,128)(2,1)S(1)} %collective-permute-done.5.p2, bf16[1056,128]{1,0:T(8,128)(2,1)S(1)} %collective-permute-done.6.p3), custom_call_target="tpu_custom_call" | custom-call | tf_op jit(solution)/shard_map/combine/pallas_call | solution.py:314
  73.9 6.3 %all-to-all-start.2 = ((bf16[32,40,128]{2,1,0:T(8,128)(2,1)}), bf16[32,40,128]{2,1,0:T(8,128)(2,1)S(1)}, u32[]{:S(2)}, u32[]{:S(2)}) async-start(bf16[32,40,128]{2,1,0:T(8,128)(2,1)} %combine.1), calls=%async_computation.2 | async-start | bytes 655360 | tf_op jit(solution)/shard_map/all_to_all | solution.py:410
  80.2 1.3 %suffix_attention.1 = (bf16[32,128]{1,0:T(8,128)(2,1)S(1)}, bf16[32,128]{1,0:T(8,128)(2,1)S(1)}, bf16[32,128]{1,0:T(8,128)(2,1)S(1)}, bf16[32,128]{1,0:T(8,128)(2,1)S(1)}) custom-call(s32[8]{0:T(128)S(1)} %copy-done.5, bf16[32,80,128]{2,1,0:T(8,128)(2,1)S(1)} %all-to-all-done.kv_own, bf16[32,80,128]{2,1,0:T(8,128)(2,1)S(1)} %collective-permute-done.7.kv_other, ...), custom_call_target="tpu_custom_call" | custom-call | flops 1048576 | bytes 65536 | tf_op jit(solution)/shard_map/suffix_attention/pallas_call | solution.py:280
  81.6 0.1 collective-permute-start.10
  81.7 3.2 %collective-permute-start.8 = (bf16[32,128]{1,0:T(8,128)(2,1)S(1)}, bf16[32,128]{1,0:T(8,128)(2,1)S(1)}, u32[]{:S(2)}, u32[]{:S(2)}) collective-permute-start(bf16[32,128]{1,0:T(8,128)(2,1)S(1)} %get-tuple-element.30), channel_id=1, source_target_pairs={{0,6},{2,0},{4,2},{6,4},{1,7},{3,1},{5,3},{7,5},{8,14},{10,8},{12,... | collective-permute-start | bytes 24584 | tf_op jit(solution)/shard_map/ppermute | solution.py:386
  84.9 1.6 %collective-permute-done.10.t3 = bf16[32,128]{1,0:T(8,128)(2,1)S(1)} collective-permute-done((bf16[32,128]{1,0:T(8,128)(2,1)S(1)}, bf16[32,128]{1,0:T(8,128)(2,1)S(1)}, u32[]{:S(2)}, u32[]{:S(2)}) %collective-permute-start.10) | collective-permute-done | bytes 8224 | tf_op jit(solution)/shard_map/ppermute | solution.py:386
  86.5 3.5 %collective-permute-done.9.t2 = bf16[32,128]{1,0:T(8,128)(2,1)S(1)} collective-permute-done((bf16[32,128]{1,0:T(8,128)(2,1)S(1)}, bf16[32,128]{1,0:T(8,128)(2,1)S(1)}, u32[]{:S(2)}, u32[]{:S(2)}) %collective-permute-start.9) | collective-permute-done | bytes 8224 | tf_op jit(solution)/shard_map/ppermute | solution.py:386
  90.0 2.5 %all-to-all-done.2.back_ref = bf16[32,40,128]{2,1,0:T(8,128)(2,1)S(1)} async-done(((bf16[32,40,128]{2,1,0:T(8,128)(2,1)}), bf16[32,40,128]{2,1,0:T(8,128)(2,1)S(1)}, u32[]{:S(2)}, u32[]{:S(2)}) %all-to-all-start.2) | async-done | bytes 327712 | tf_op jit(solution)/shard_map/all_to_all | solution.py:410
  92.5 1.7 %finish.1 = bf16[8,4,256]{2,1,0:T(4,128)(2,1)} custom-call(s32[8]{0:T(128)S(1)} %bitcast.7, s32[8]{0:T(128)S(1)} %copy-done.4, bf16[32,40,128]{2,1,0:T(8,128)(2,1)S(1)} %all-to-all-done.2.back_ref, bf16[32,128]{1,0:T(8,128)(2,1)S(1)} %get-tuple-element.29.t0, bf16[32,128]{1,0:T(8,128)(2,1)S(1)} %collective-permute-done.8.t1, ...), custom_call_target="tpu_custom_call" | custom-call | tf_op jit(solution)/shard_map/finish/pallas_call | solution.py:368
  (13 shorter events, 0.0 us)
Async XLA Ops:
  0.0 25.0 %collective-permute-start = (bf16[2,1024,2048]{2,1,0:T(8,128)(2,1)}, bf16[2,1024,2048]{2,1,0:T(8,128)(2,1)}, u32[]{:S(2)}, u32[]{:S(2)}) collective-permute-start(bf16[2,1024,2048]{2,1,0:T(8,128)(2,1)} %own.1), channel_id=1, source_target_pairs={{0,1},{1,0},{2,3},{3,2},{4,5},{5,4},{6,7},{7,6},{8,9},{9,8},{10,11... | collective-permute-start | bytes 25165832 | tf_op jit(solution)/shard_map/ppermute | solution.py:390
  25.0 12.6 %collective-permute-start.1 = (bf16[1024,128]{1,0:T(8,128)(2,1)S(1)}, bf16[1024,128]{1,0:T(8,128)(2,1)S(1)}, u32[]{:S(2)}, u32[]{:S(2)}) collective-permute-start(bf16[1024,128]{1,0:T(8,128)(2,1)S(1)} %bitcast.2), channel_id=1, source_target_pairs={{0,2},{2,4},{4,6},{6,0},{1,3},{3,5},{5,7},{7,1},{8,10},{10,12},{12... | collective-permute-start | bytes 786440 | tf_op jit(solution)/shard_map/ppermute | solution.py:386
  26.6 14.4 %collective-permute-start.2 = (bf16[1024,128]{1,0:T(8,128)(2,1)S(1)}, bf16[1024,128]{1,0:T(8,128)(2,1)S(1)}, u32[]{:S(2)}, u32[]{:S(2)}) collective-permute-start(bf16[1024,128]{1,0:T(8,128)(2,1)S(1)} %bitcast.3), channel_id=1, source_target_pairs={{0,4},{2,6},{4,0},{6,2},{1,5},{3,7},{5,1},{7,3},{8,12},{10,14},{12... | collective-permute-start | bytes 786440 | tf_op jit(solution)/shard_map/ppermute | solution.py:386
  29.5 11.5 %collective-permute-start.3 = (bf16[1024,128]{1,0:T(8,128)(2,1)S(1)}, bf16[1024,128]{1,0:T(8,128)(2,1)S(1)}, u32[]{:S(2)}, u32[]{:S(2)}) collective-permute-start(bf16[1024,128]{1,0:T(8,128)(2,1)S(1)} %bitcast.4), channel_id=1, source_target_pairs={{0,6},{2,0},{4,2},{6,4},{1,7},{3,1},{5,3},{7,5},{8,14},{10,8},{12,... | collective-permute-start | bytes 786440 | tf_op jit(solution)/shard_map/ppermute | solution.py:386
  30.8 1.0 %copy-start = (bf16[8,16,2048]{2,1,0:T(8,128)(2,1)S(1)}, bf16[8,16,2048]{2,1,0:T(8,128)(2,1)}, u32[]{:S(2)}) copy-start(bf16[8,16,2048]{2,1,0:T(8,128)(2,1)} %kv_ref.1) | copy-start | bytes 1572868
  31.9 0.7 copy-start.2
  33.6 26.6 %all-to-all-start = ((bf16[32,80,128]{2,1,0:T(8,128)(2,1)}), bf16[32,80,128]{2,1,0:T(8,128)(2,1)S(1)}, u32[]{:S(2)}, u32[]{:S(2)}) async-start(bf16[32,80,128]{2,1,0:T(8,128)(2,1)} %pack_suffix.1), calls=%async_computation | async-start | bytes 1310720 | tf_op jit(solution)/shard_map/all_to_all | solution.py:402
  37.5 42.7 %copy-start.1 = (bf16[8,4,2048]{2,1,0:T(4,128)(2,1)S(1)}, bf16[8,4,2048]{2,1,0:T(4,128)(2,1)}, u32[]{:S(2)}) copy-start(bf16[8,4,2048]{2,1,0:T(4,128)(2,1)} %new_kv.1) | copy-start | bytes 393220
  37.5 42.7 %copy-start.5 = (s32[8]{0:T(128)S(1)}, s32[8]{0:T(128)}, u32[]{:S(2)}) copy-start(s32[8]{0:T(128)} %len_ref.1) | copy-start | bytes 100
  37.5 55.0 %copy-start.3 = (s32[8,1]{0,1:T(1,128)S(1)}, s32[8,1]{0,1:T(1,128)}, u32[]{:S(2)}) copy-start(s32[8,1]{0,1:T(1,128)} %param.11) | copy-start | bytes 100
  37.6 55.0 %copy-start.4 = (s32[8]{0:T(128)S(1)}, s32[8]{0:T(128)}, u32[]{:S(2)}) copy-start(s32[8]{0:T(128)} %place_ref.3) | copy-start | bytes 100
  56.1 13.4 %collective-permute-start.4 = (bf16[1056,128]{1,0:T(8,128)(2,1)S(1)}, bf16[1056,128]{1,0:T(8,128)(2,1)S(1)}, u32[]{:S(2)}, u32[]{:S(2)}) collective-permute-start(bf16[1056,128]{1,0:T(8,128)(2,1)S(1)} %get-tuple-element.25), channel_id=1, source_target_pairs={{0,6},{2,0},{4,2},{6,4},{1,7},{3,1},{5,3},{7,5},{8,14},{10,8},{12,... | collective-permute-start | bytes 811016 | tf_op jit(solution)/shard_map/ppermute | solution.py:386
  58.4 11.0 %collective-permute-start.5 = (bf16[1056,128]{1,0:T(8,128)(2,1)S(1)}, bf16[1056,128]{1,0:T(8,128)(2,1)S(1)}, u32[]{:S(2)}, u32[]{:S(2)}) collective-permute-start(bf16[1056,128]{1,0:T(8,128)(2,1)S(1)} %get-tuple-element.26), channel_id=1, source_target_pairs={{0,4},{2,6},{4,0},{6,2},{1,5},{3,7},{5,1},{7,3},{8,12},{10,14},{12... | collective-permute-start | bytes 811016 | tf_op jit(solution)/shard_map/ppermute | solution.py:386
  59.4 13.6 %collective-permute-start.6 = (bf16[1056,128]{1,0:T(8,128)(2,1)S(1)}, bf16[1056,128]{1,0:T(8,128)(2,1)S(1)}, u32[]{:S(2)}, u32[]{:S(2)}) collective-permute-start(bf16[1056,128]{1,0:T(8,128)(2,1)S(1)} %get-tuple-element.27), channel_id=1, source_target_pairs={{0,2},{2,4},{4,6},{6,0},{1,3},{3,5},{5,7},{7,1},{8,10},{10,12},{12... | collective-permute-start | bytes 811016 | tf_op jit(solution)/shard_map/ppermute | solution.py:386
  60.2 20.0 %collective-permute-start.7 = (bf16[32,80,128]{2,1,0:T(8,128)(2,1)S(1)}, bf16[32,80,128]{2,1,0:T(8,128)(2,1)S(1)}, u32[]{:S(2)}, u32[]{:S(2)}) collective-permute-start(bf16[32,80,128]{2,1,0:T(8,128)(2,1)S(1)} %all-to-all-done.kv_own), channel_id=1, source_target_pairs={{0,1},{1,0},{2,3},{3,2},{4,5},{5,4},{6,7},{7,6},{8,9},{9,8},{10,11... | collective-permute-start | bytes 1966088 | tf_op jit(solution)/shard_map/ppermute | solution.py:390
  73.9 18.6 %all-to-all-start.2 = ((bf16[32,40,128]{2,1,0:T(8,128)(2,1)}), bf16[32,40,128]{2,1,0:T(8,128)(2,1)S(1)}, u32[]{:S(2)}, u32[]{:S(2)}) async-start(bf16[32,40,128]{2,1,0:T(8,128)(2,1)} %combine.1), calls=%async_computation.2 | async-start | bytes 655360 | tf_op jit(solution)/shard_map/all_to_all | solution.py:410
  81.6 4.9 %collective-permute-start.10 = (bf16[32,128]{1,0:T(8,128)(2,1)S(1)}, bf16[32,128]{1,0:T(8,128)(2,1)S(1)}, u32[]{:S(2)}, u32[]{:S(2)}) collective-permute-start(bf16[32,128]{1,0:T(8,128)(2,1)S(1)} %get-tuple-element.32), channel_id=1, source_target_pairs={{0,2},{2,4},{4,6},{6,0},{1,3},{3,5},{5,7},{7,1},{8,10},{10,12},{12... | collective-permute-start | bytes 24584 | tf_op jit(solution)/shard_map/ppermute | solution.py:386
  81.7 4.9 %collective-permute-start.8 = (bf16[32,128]{1,0:T(8,128)(2,1)S(1)}, bf16[32,128]{1,0:T(8,128)(2,1)S(1)}, u32[]{:S(2)}, u32[]{:S(2)}) collective-permute-start(bf16[32,128]{1,0:T(8,128)(2,1)S(1)} %get-tuple-element.30), channel_id=1, source_target_pairs={{0,6},{2,0},{4,2},{6,4},{1,7},{3,1},{5,3},{7,5},{8,14},{10,8},{12,... | collective-permute-start | bytes 24584 | tf_op jit(solution)/shard_map/ppermute | solution.py:386
  84.9 5.2 %collective-permute-start.9 = (bf16[32,128]{1,0:T(8,128)(2,1)S(1)}, bf16[32,128]{1,0:T(8,128)(2,1)S(1)}, u32[]{:S(2)}, u32[]{:S(2)}) collective-permute-start(bf16[32,128]{1,0:T(8,128)(2,1)S(1)} %get-tuple-element.31), channel_id=1, source_target_pairs={{0,4},{2,6},{4,0},{6,2},{1,5},{3,7},{5,1},{7,3},{8,12},{10,14},{12... | collective-permute-start | bytes 24584 | tf_op jit(solution)/shard_map/ppermute | solution.py:386
where the time goes:
time: 95.2 us; the launch traced here: 94.2 us
  waiting for transfers between devices  23.8 us (25%)
  blocking collectives  23.5 us (25%)
  starting transfers between devices  23.4 us (25%)
  Pallas kernels  21.7 us (23%)
  local copies, waits for them, and re-layouts  1.78 us (2%)
    all_to_all x1, blocking collectives, per_device(): arrived = lax.all_to_all(send, ('z', 'grp'), 0, 0, tiled=True)  23.5 us
    ppermute x9, waiting for transfers between devices, turn(): return lax.ppermute(x, 'y', [(i, (i + by) % NY) for i in range(NY)])  21.3 us
    pallas_call x1, Pallas kernels, prefix_attention(): pl.pallas_call(prefix_kernel, out_shape=(jax.ShapeDtypeStruct((ROWS, HD),...  15.1 us
    ppermute x9, starting transfers between devices, turn(): return lax.ppermute(x, 'y', [(i, (i + by) % NY) for i in range(NY)])  13.2 us
    all_to_all x1, starting transfers between devices, per_device(): back = lax.all_to_all(joined, ('z', 'grp'), 0, 0, tiled=True)  6.27 us
    all_to_all x1, starting transfers between devices, per_device(): suffix_own = lax.all_to_all(packed, ('y', 'z'), 0, 0, tiled=True)  3.9 us
    all_to_all x1, waiting for transfers between devices, per_device(): back = lax.all_to_all(joined, ('z', 'grp'), 0, 0, tiled=True)  2.49 us
  transfers between devices with their start and end apart: 13, of which 6 were waited for; matrix products, arithmetic and copies ran while one was open for 0% of the time, Pallas kernels for 21%

commit v1 on v0

--- a/solution.py
+++ b/solution.py
@@ -14,7 +14,7 @@
 REQ = 8
 SPAN = 16
 HALF = 1024
-STATS = 32
+STATS = 16
 ROWS = NZ * HD + STATS
 TAIL = 32
 MESSAGE = 4 * SPAN + 16
@@ -139,8 +139,7 @@
             total = total + jnp.sum(w.reshape(CHUNK // 8, 8, 256), axis=0)
             v = kv[p, start : start + CHUNK, lanes(NZ + z)]
             summed = summed + tn_dot(v, w.astype(BF16))
-    high, low = split_total(jnp.sum(total, axis=0, keepdims=True))
-    return summed, (top, high, low)
+    return summed, (top, jnp.sum(total, axis=0, keepdims=True))
 
 
 def prefix_kernel(q0, q1, q2, q3, own, other, o0, o1, o2, o3, kv0, kv1, sa, sb, ma, mb, stats, sems):
@@ -171,7 +170,7 @@
         for k, out in enumerate((o0, o1, o2, o3)):
             cols = slice(64 * k, 64 * (k + 1))
             out[rows, :] = jnp.concatenate([even[0][:, cols], odd[0][:, cols]], axis=1).astype(BF16)
-            for i in range(3):
+            for i in range(2):
                 stats[k, pl.ds(8 * i + z, 1), :] = jnp.concatenate(
                     [even[1][i][:, cols], odd[1][i][:, cols]], axis=1
                 )
@@ -292,7 +291,7 @@
     stats = [ref[NZ * HD :, :].astype(F32) for ref in (p0, p1, p2, p3)]
     top = functools.reduce(jnp.maximum, [s[:NZ] for s in stats])
     factors = [jnp.exp2(s[:NZ] - top) for s in stats]
-    total = sum((s[NZ : 2 * NZ] + s[2 * NZ : 3 * NZ]) * f for s, f in zip(stats, factors))
+    total = sum(s[NZ : 2 * NZ] * f for s, f in zip(stats, factors))
     high, low = split_total(total)
     row = lax.broadcasted_iota(jnp.int32, (8, HD), 0)
     for z in range(NZ):

time: 95.2 us -> 94.6 us (level)
  no operation moved by 1% of the time
where the time goes in v1:
time: 94.6 us; the launch traced here: 93.7 us
  waiting for transfers between devices  23.6 us (25%)
  blocking collectives  23.5 us (25%)
  starting transfers between devices  23.4 us (25%)
  Pallas kernels  21.4 us (23%)
  local copies, waits for them, and re-layouts  1.78 us (2%)
    all_to_all x1, blocking collectives, per_device(): arrived = lax.all_to_all(send, ('z', 'grp'), 0, 0, tiled=True)  23.5 us
    ppermute x9, waiting for transfers between devices, turn(): return lax.ppermute(x, 'y', [(i, (i + by) % NY) for i in range(NY)])  21.1 us
    pallas_call x1, Pallas kernels, prefix_attention(): pl.pallas_call(prefix_kernel, out_shape=(jax.ShapeDtypeStruct((ROWS, HD),...  14.8 us
    ppermute x9, starting transfers between devices, turn(): return lax.ppermute(x, 'y', [(i, (i + by) % NY) for i in range(NY)])  13.2 us
    all_to_all x1, starting transfers between devices, per_device(): back = lax.all_to_all(joined, ('z', 'grp'), 0, 0, tiled=True)  6.27 us
    all_to_all x1, starting transfers between devices, per_device(): suffix_own = lax.all_to_all(packed, ('y', 'z'), 0, 0, tiled=True)  3.9 us
    all_to_all x1, waiting for transfers between devices, per_device(): back = lax.all_to_all(joined, ('z', 'grp'), 0, 0, tiled=True)  2.45 us
  transfers between devices with their start and end apart: 13, of which 6 were waited for; matrix products, arithmetic and copies ran while one was open for 0% of the time, Pallas kernels for 21%

profile of v1, /device:TPU:4, one launch (start us, length us, event | category | flops | bytes accessed | tf_op | source)
XLA Modules:
  0.0 93.7 jit_solution(3866313183690498224)
XLA Ops:
  0.0 0.0 collective-permute-start
  0.0 1.5 %pack_queries.1 = (bf16[32,32,128]{2,1,0:T(8,128)(2,1)}, bf16[4,16,128]{2,1,0:T(8,128)(2,1)}) custom-call(s32[8]{0:T(128)} %bitcast.6, s32[8]{0:T(128)} %place_ref.3, bf16[8,4,256]{2,1,0:T(4,128)(2,1)} %q_ref.1), custom_call_target="tpu_custom_call" | custom-call | tf_op jit(solution)/shard_map/pack_queries/pallas_call | solution.py:64
  1.5 23.5 %all_to_all.15 = bf16[32,32,128]{2,1,0:T(8,128)(2,1)S(1)} all-to-all(bf16[32,32,128]{2,1,0:T(8,128)(2,1)} %get-tuple-element.20), channel_id=1, replica_groups=mesh['grp'=4,'z'=8,'y'=4,'c'=2] {'z','grp'}, dimensions={0} | all-to-all | bytes 524288 | tf_op jit(solution)/shard_map/all_to_all | solution.py:397
  25.0 0.0 collective-permute-done.other
  25.0 1.6 %collective-permute-start.1 = (bf16[1024,128]{1,0:T(8,128)(2,1)S(1)}, bf16[1024,128]{1,0:T(8,128)(2,1)S(1)}, u32[]{:S(2)}, u32[]{:S(2)}) collective-permute-start(bf16[1024,128]{1,0:T(8,128)(2,1)S(1)} %bitcast.2), channel_id=1, source_target_pairs={{0,2},{2,4},{4,6},{6,0},{1,3},{3,5},{5,7},{7,1},{8,10},{10,12},{12... | collective-permute-start | bytes 786440 | tf_op jit(solution)/shard_map/ppermute | solution.py:385
  26.6 2.9 %collective-permute-start.2 = (bf16[1024,128]{1,0:T(8,128)(2,1)S(1)}, bf16[1024,128]{1,0:T(8,128)(2,1)S(1)}, u32[]{:S(2)}, u32[]{:S(2)}) collective-permute-start(bf16[1024,128]{1,0:T(8,128)(2,1)S(1)} %bitcast.3), channel_id=1, source_target_pairs={{0,4},{2,6},{4,0},{6,2},{1,5},{3,7},{5,1},{7,3},{8,12},{10,14},{12... | collective-permute-start | bytes 786440 | tf_op jit(solution)/shard_map/ppermute | solution.py:385
  29.5 1.3 %collective-permute-start.3 = (bf16[1024,128]{1,0:T(8,128)(2,1)S(1)}, bf16[1024,128]{1,0:T(8,128)(2,1)S(1)}, u32[]{:S(2)}, u32[]{:S(2)}) collective-permute-start(bf16[1024,128]{1,0:T(8,128)(2,1)S(1)} %bitcast.4), channel_id=1, source_target_pairs={{0,6},{2,0},{4,2},{6,4},{1,7},{3,1},{5,3},{7,5},{8,14},{10,8},{12,... | collective-permute-start | bytes 786440 | tf_op jit(solution)/shard_map/ppermute | solution.py:385
  30.8 1.0 %copy-done = bf16[8,16,2048]{2,1,0:T(8,128)(2,1)S(1)} copy-done((bf16[8,16,2048]{2,1,0:T(8,128)(2,1)S(1)}, bf16[8,16,2048]{2,1,0:T(8,128)(2,1)}, u32[]{:S(2)}) %copy-start) | copy-done | bytes 524312
  31.9 0.7 copy-done.2
  32.6 1.0 %pack_suffix.1 = bf16[32,80,128]{2,1,0:T(8,128)(2,1)} custom-call(bf16[8,16,2048]{2,1,0:T(8,128)(2,1)S(1)} %copy-done, bf16[4,16,128]{2,1,0:T(8,128)(2,1)S(1)} %copy-done.2), custom_call_target="tpu_custom_call" | custom-call | tf_op jit(solution)/shard_map/pack_suffix/pallas_call | solution.py:98
  33.6 3.9 %all-to-all-start = ((bf16[32,80,128]{2,1,0:T(8,128)(2,1)}), bf16[32,80,128]{2,1,0:T(8,128)(2,1)S(1)}, u32[]{:S(2)}, u32[]{:S(2)}) async-start(bf16[32,80,128]{2,1,0:T(8,128)(2,1)} %pack_suffix.1), calls=%async_computation | async-start | bytes 1310720 | tf_op jit(solution)/shard_map/all_to_all | solution.py:401
  37.5 0.0 copy-start.1
  37.5 0.0 copy-start.5
  37.5 0.0 copy-start.3
  37.6 0.0 copy-start.4
  37.6 3.4 %collective-permute-done.2.q2 = bf16[1024,128]{1,0:T(8,128)(2,1)S(1)} collective-permute-done((bf16[1024,128]{1,0:T(8,128)(2,1)S(1)}, bf16[1024,128]{1,0:T(8,128)(2,1)S(1)}, u32[]{:S(2)}, u32[]{:S(2)}) %collective-permute-start.2) | collective-permute-done | bytes 262176 | tf_op jit(solution)/shard_map/ppermute | solution.py:385
  40.9 14.8 %prefix_attention.1 = (bf16[1040,128]{1,0:T(8,128)(2,1)S(1)}, bf16[1040,128]{1,0:T(8,128)(2,1)S(1)}, bf16[1040,128]{1,0:T(8,128)(2,1)S(1)}, bf16[1040,128]{1,0:T(8,128)(2,1)S(1)}) custom-call(bf16[1024,128]{1,0:T(8,128)(2,1)S(1)} %bitcast.5, bf16[1024,128]{1,0:T(8,128)(2,1)S(1)} %collective-permute-done.1.q1, ...), custom_call_target="tpu_custom_call" | custom-call | flops 21474836480 | bytes 18874368 | tf_op jit(solution)/shard_map/prefix_attention/pallas_call | solution.py:198
  55.8 2.4 %collective-permute-start.4 = (bf16[1040,128]{1,0:T(8,128)(2,1)S(1)}, bf16[1040,128]{1,0:T(8,128)(2,1)S(1)}, u32[]{:S(2)}, u32[]{:S(2)}) collective-permute-start(bf16[1040,128]{1,0:T(8,128)(2,1)S(1)} %get-tuple-element.25), channel_id=1, source_target_pairs={{0,6},{2,0},{4,2},{6,4},{1,7},{3,1},{5,3},{7,5},{8,14},{10,8},{12,... | collective-permute-start | bytes 798728 | tf_op jit(solution)/shard_map/ppermute | solution.py:385
  58.1 0.9 collective-permute-start.5
  59.0 0.8 collective-permute-start.6
  59.8 0.0 all-to-all-done.kv_own
  59.8 9.1 %collective-permute-done.4.p1 = bf16[1040,128]{1,0:T(8,128)(2,1)S(1)} collective-permute-done((bf16[1040,128]{1,0:T(8,128)(2,1)S(1)}, bf16[1040,128]{1,0:T(8,128)(2,1)S(1)}, u32[]{:S(2)}, u32[]{:S(2)}) %collective-permute-start.4) | collective-permute-done | bytes 266272 | tf_op jit(solution)/shard_map/ppermute | solution.py:385
  69.0 3.4 %collective-permute-done.6.p3 = bf16[1040,128]{1,0:T(8,128)(2,1)S(1)} collective-permute-done((bf16[1040,128]{1,0:T(8,128)(2,1)S(1)}, bf16[1040,128]{1,0:T(8,128)(2,1)S(1)}, u32[]{:S(2)}, u32[]{:S(2)}) %collective-permute-start.6) | collective-permute-done | bytes 266272 | tf_op jit(solution)/shard_map/ppermute | solution.py:385
  72.4 1.0 %combine.1 = bf16[32,40,128]{2,1,0:T(8,128)(2,1)} custom-call(bf16[1040,128]{1,0:T(8,128)(2,1)S(1)} %get-tuple-element.24.p0, bf16[1040,128]{1,0:T(8,128)(2,1)S(1)} %collective-permute-done.4.p1, bf16[1040,128]{1,0:T(8,128)(2,1)S(1)} %collective-permute-done.5.p2, bf16[1040,128]{1,0:T(8,128)(2,1)S(1)} %collective-permute-done.6.p3), custom_call_target="tpu_custom_call" | custom-call | tf_op jit(solution)/shard_map/combine/pallas_call | solution.py:313
  73.4 6.3 %all-to-all-start.2 = ((bf16[32,40,128]{2,1,0:T(8,128)(2,1)}), bf16[32,40,128]{2,1,0:T(8,128)(2,1)S(1)}, u32[]{:S(2)}, u32[]{:S(2)}) async-start(bf16[32,40,128]{2,1,0:T(8,128)(2,1)} %combine.1), calls=%async_computation.2 | async-start | bytes 655360 | tf_op jit(solution)/shard_map/all_to_all | solution.py:409
  79.7 1.3 %suffix_attention.1 = (bf16[32,128]{1,0:T(8,128)(2,1)S(1)}, bf16[32,128]{1,0:T(8,128)(2,1)S(1)}, bf16[32,128]{1,0:T(8,128)(2,1)S(1)}, bf16[32,128]{1,0:T(8,128)(2,1)S(1)}) custom-call(s32[8]{0:T(128)S(1)} %copy-done.5, bf16[32,80,128]{2,1,0:T(8,128)(2,1)S(1)} %all-to-all-done.kv_own, bf16[32,80,128]{2,1,0:T(8,128)(2,1)S(1)} %collective-permute-done.7.kv_other, ...), custom_call_target="tpu_custom_call" | custom-call | flops 1048576 | bytes 65536 | tf_op jit(solution)/shard_map/suffix_attention/pallas_call | solution.py:279
  81.1 0.1 collective-permute-start.10
  81.2 3.2 %collective-permute-start.8 = (bf16[32,128]{1,0:T(8,128)(2,1)S(1)}, bf16[32,128]{1,0:T(8,128)(2,1)S(1)}, u32[]{:S(2)}, u32[]{:S(2)}) collective-permute-start(bf16[32,128]{1,0:T(8,128)(2,1)S(1)} %get-tuple-element.30), channel_id=1, source_target_pairs={{0,6},{2,0},{4,2},{6,4},{1,7},{3,1},{5,3},{7,5},{8,14},{10,8},{12,... | collective-permute-start | bytes 24584 | tf_op jit(solution)/shard_map/ppermute | solution.py:385
  84.4 1.6 %collective-permute-done.10.t3 = bf16[32,128]{1,0:T(8,128)(2,1)S(1)} collective-permute-done((bf16[32,128]{1,0:T(8,128)(2,1)S(1)}, bf16[32,128]{1,0:T(8,128)(2,1)S(1)}, u32[]{:S(2)}, u32[]{:S(2)}) %collective-permute-start.10) | collective-permute-done | bytes 8224 | tf_op jit(solution)/shard_map/ppermute | solution.py:385
  86.0 3.5 %collective-permute-done.9.t2 = bf16[32,128]{1,0:T(8,128)(2,1)S(1)} collective-permute-done((bf16[32,128]{1,0:T(8,128)(2,1)S(1)}, bf16[32,128]{1,0:T(8,128)(2,1)S(1)}, u32[]{:S(2)}, u32[]{:S(2)}) %collective-permute-start.9) | collective-permute-done | bytes 8224 | tf_op jit(solution)/shard_map/ppermute | solution.py:385
  89.5 2.4 %all-to-all-done.2.back_ref = bf16[32,40,128]{2,1,0:T(8,128)(2,1)S(1)} async-done(((bf16[32,40,128]{2,1,0:T(8,128)(2,1)}), bf16[32,40,128]{2,1,0:T(8,128)(2,1)S(1)}, u32[]{:S(2)}, u32[]{:S(2)}) %all-to-all-start.2) | async-done | bytes 327712 | tf_op jit(solution)/shard_map/all_to_all | solution.py:409
  92.0 1.7 %finish.1 = bf16[8,4,256]{2,1,0:T(4,128)(2,1)} custom-call(s32[8]{0:T(128)S(1)} %bitcast.7, s32[8]{0:T(128)S(1)} %copy-done.4, bf16[32,40,128]{2,1,0:T(8,128)(2,1)S(1)} %all-to-all-done.2.back_ref, bf16[32,128]{1,0:T(8,128)(2,1)S(1)} %get-tuple-element.29.t0, bf16[32,128]{1,0:T(8,128)(2,1)S(1)} %collective-permute-done.8.t1, ...), custom_call_target="tpu_custom_call" | custom-call | tf_op jit(solution)/shard_map/finish/pallas_call | solution.py:367
  (13 shorter events, 0.0 us)
Async XLA Ops:
  0.0 25.0 %collective-permute-start = (bf16[2,1024,2048]{2,1,0:T(8,128)(2,1)}, bf16[2,1024,2048]{2,1,0:T(8,128)(2,1)}, u32[]{:S(2)}, u32[]{:S(2)}) collective-permute-start(bf16[2,1024,2048]{2,1,0:T(8,128)(2,1)} %own.1), channel_id=1, source_target_pairs={{0,1},{1,0},{2,3},{3,2},{4,5},{5,4},{6,7},{7,6},{8,9},{9,8},{10,11... | collective-permute-start | bytes 25165832 | tf_op jit(solution)/shard_map/ppermute | solution.py:389
  25.0 12.6 %collective-permute-start.1 = (bf16[1024,128]{1,0:T(8,128)(2,1)S(1)}, bf16[1024,128]{1,0:T(8,128)(2,1)S(1)}, u32[]{:S(2)}, u32[]{:S(2)}) collective-permute-start(bf16[1024,128]{1,0:T(8,128)(2,1)S(1)} %bitcast.2), channel_id=1, source_target_pairs={{0,2},{2,4},{4,6},{6,0},{1,3},{3,5},{5,7},{7,1},{8,10},{10,12},{12... | collective-permute-start | bytes 786440 | tf_op jit(solution)/shard_map/ppermute | solution.py:385
  26.6 14.4 %collective-permute-start.2 = (bf16[1024,128]{1,0:T(8,128)(2,1)S(1)}, bf16[1024,128]{1,0:T(8,128)(2,1)S(1)}, u32[]{:S(2)}, u32[]{:S(2)}) collective-permute-start(bf16[1024,128]{1,0:T(8,128)(2,1)S(1)} %bitcast.3), channel_id=1, source_target_pairs={{0,4},{2,6},{4,0},{6,2},{1,5},{3,7},{5,1},{7,3},{8,12},{10,14},{12... | collective-permute-start | bytes 786440 | tf_op jit(solution)/shard_map/ppermute | solution.py:385
  29.5 11.5 %collective-permute-start.3 = (bf16[1024,128]{1,0:T(8,128)(2,1)S(1)}, bf16[1024,128]{1,0:T(8,128)(2,1)S(1)}, u32[]{:S(2)}, u32[]{:S(2)}) collective-permute-start(bf16[1024,128]{1,0:T(8,128)(2,1)S(1)} %bitcast.4), channel_id=1, source_target_pairs={{0,6},{2,0},{4,2},{6,4},{1,7},{3,1},{5,3},{7,5},{8,14},{10,8},{12,... | collective-permute-start | bytes 786440 | tf_op jit(solution)/shard_map/ppermute | solution.py:385
  30.8 1.0 %copy-start = (bf16[8,16,2048]{2,1,0:T(8,128)(2,1)S(1)}, bf16[8,16,2048]{2,1,0:T(8,128)(2,1)}, u32[]{:S(2)}) copy-start(bf16[8,16,2048]{2,1,0:T(8,128)(2,1)} %kv_ref.1) | copy-start | bytes 1572868
  31.9 0.7 copy-start.2
  33.6 26.2 %all-to-all-start = ((bf16[32,80,128]{2,1,0:T(8,128)(2,1)}), bf16[32,80,128]{2,1,0:T(8,128)(2,1)S(1)}, u32[]{:S(2)}, u32[]{:S(2)}) async-start(bf16[32,80,128]{2,1,0:T(8,128)(2,1)} %pack_suffix.1), calls=%async_computation | async-start | bytes 1310720 | tf_op jit(solution)/shard_map/all_to_all | solution.py:401
  37.5 42.2 %copy-start.1 = (bf16[8,4,2048]{2,1,0:T(4,128)(2,1)S(1)}, bf16[8,4,2048]{2,1,0:T(4,128)(2,1)}, u32[]{:S(2)}) copy-start(bf16[8,4,2048]{2,1,0:T(4,128)(2,1)} %new_kv.1) | copy-start | bytes 393220
  37.5 42.2 %copy-start.5 = (s32[8]{0:T(128)S(1)}, s32[8]{0:T(128)}, u32[]{:S(2)}) copy-start(s32[8]{0:T(128)} %len_ref.1) | copy-start | bytes 100
  37.5 54.4 %copy-start.3 = (s32[8,1]{0,1:T(1,128)S(1)}, s32[8,1]{0,1:T(1,128)}, u32[]{:S(2)}) copy-start(s32[8,1]{0,1:T(1,128)} %param.11) | copy-start | bytes 100
  37.6 54.4 %copy-start.4 = (s32[8]{0:T(128)S(1)}, s32[8]{0:T(128)}, u32[]{:S(2)}) copy-start(s32[8]{0:T(128)} %place_ref.3) | copy-start | bytes 100
  55.8 13.2 %collective-permute-start.4 = (bf16[1040,128]{1,0:T(8,128)(2,1)S(1)}, bf16[1040,128]{1,0:T(8,128)(2,1)S(1)}, u32[]{:S(2)}, u32[]{:S(2)}) collective-permute-start(bf16[1040,128]{1,0:T(8,128)(2,1)S(1)} %get-tuple-element.25), channel_id=1, source_target_pairs={{0,6},{2,0},{4,2},{6,4},{1,7},{3,1},{5,3},{7,5},{8,14},{10,8},{12,... | collective-permute-start | bytes 798728 | tf_op jit(solution)/shard_map/ppermute | solution.py:385
  58.1 10.9 %collective-permute-start.5 = (bf16[1040,128]{1,0:T(8,128)(2,1)S(1)}, bf16[1040,128]{1,0:T(8,128)(2,1)S(1)}, u32[]{:S(2)}, u32[]{:S(2)}) collective-permute-start(bf16[1040,128]{1,0:T(8,128)(2,1)S(1)} %get-tuple-element.26), channel_id=1, source_target_pairs={{0,4},{2,6},{4,0},{6,2},{1,5},{3,7},{5,1},{7,3},{8,12},{10,14},{12... | collective-permute-start | bytes 798728 | tf_op jit(solution)/shard_map/ppermute | solution.py:385
  59.0 13.4 %collective-permute-start.6 = (bf16[1040,128]{1,0:T(8,128)(2,1)S(1)}, bf16[1040,128]{1,0:T(8,128)(2,1)S(1)}, u32[]{:S(2)}, u32[]{:S(2)}) collective-permute-start(bf16[1040,128]{1,0:T(8,128)(2,1)S(1)} %get-tuple-element.27), channel_id=1, source_target_pairs={{0,2},{2,4},{4,6},{6,0},{1,3},{3,5},{5,7},{7,1},{8,10},{10,12},{12... | collective-permute-start | bytes 798728 | tf_op jit(solution)/shard_map/ppermute | solution.py:385
  59.8 19.9 %collective-permute-start.7 = (bf16[32,80,128]{2,1,0:T(8,128)(2,1)S(1)}, bf16[32,80,128]{2,1,0:T(8,128)(2,1)S(1)}, u32[]{:S(2)}, u32[]{:S(2)}) collective-permute-start(bf16[32,80,128]{2,1,0:T(8,128)(2,1)S(1)} %all-to-all-done.kv_own), channel_id=1, source_target_pairs={{0,1},{1,0},{2,3},{3,2},{4,5},{5,4},{6,7},{7,6},{8,9},{9,8},{10,11... | collective-permute-start | bytes 1966088 | tf_op jit(solution)/shard_map/ppermute | solution.py:389
  73.4 18.6 %all-to-all-start.2 = ((bf16[32,40,128]{2,1,0:T(8,128)(2,1)}), bf16[32,40,128]{2,1,0:T(8,128)(2,1)S(1)}, u32[]{:S(2)}, u32[]{:S(2)}) async-start(bf16[32,40,128]{2,1,0:T(8,128)(2,1)} %combine.1), calls=%async_computation.2 | async-start | bytes 655360 | tf_op jit(solution)/shard_map/all_to_all | solution.py:409
  81.1 4.9 %collective-permute-start.10 = (bf16[32,128]{1,0:T(8,128)(2,1)S(1)}, bf16[32,128]{1,0:T(8,128)(2,1)S(1)}, u32[]{:S(2)}, u32[]{:S(2)}) collective-permute-start(bf16[32,128]{1,0:T(8,128)(2,1)S(1)} %get-tuple-element.32), channel_id=1, source_target_pairs={{0,2},{2,4},{4,6},{6,0},{1,3},{3,5},{5,7},{7,1},{8,10},{10,12},{12... | collective-permute-start | bytes 24584 | tf_op jit(solution)/shard_map/ppermute | solution.py:385
  81.2 4.9 %collective-permute-start.8 = (bf16[32,128]{1,0:T(8,128)(2,1)S(1)}, bf16[32,128]{1,0:T(8,128)(2,1)S(1)}, u32[]{:S(2)}, u32[]{:S(2)}) collective-permute-start(bf16[32,128]{1,0:T(8,128)(2,1)S(1)} %get-tuple-element.30), channel_id=1, source_target_pairs={{0,6},{2,0},{4,2},{6,4},{1,7},{3,1},{5,3},{7,5},{8,14},{10,8},{12,... | collective-permute-start | bytes 24584 | tf_op jit(solution)/shard_map/ppermute | solution.py:385
  84.4 5.2 %collective-permute-start.9 = (bf16[32,128]{1,0:T(8,128)(2,1)S(1)}, bf16[32,128]{1,0:T(8,128)(2,1)S(1)}, u32[]{:S(2)}, u32[]{:S(2)}) collective-permute-start(bf16[32,128]{1,0:T(8,128)(2,1)S(1)} %get-tuple-element.31), channel_id=1, source_target_pairs={{0,4},{2,6},{4,0},{6,2},{1,5},{3,7},{5,1},{7,3},{8,12},{10,14},{12... | collective-permute-start | bytes 24584 | tf_op jit(solution)/shard_map/ppermute | solution.py:385
